TPU v7x, 32 devices: a whole 2x2x4 slice. The times are simulated.
32 devices in a mesh: grp: 4 (over y, core), pair: 8 (over z, x).
Axes of the slice: x: 2, y: 2, z: 4, core: 2. Of those that a mesh axis runs over, the one named last changes fastest.
Arguments:
- integrals: bfloat16 [64, 2000, 2000], P('pair', 'grp'), may hold values from -6 to 6
- coeff: bfloat16 [2000, 96], replicated, may hold values from -0.125 to 0.125
- mu_index: int32 [64], replicated, may hold values from 0 to 1999
- nu_index: int32 [64], replicated, may hold values from 0 to 7
- ao_irrep: int32 [8], replicated, may hold values from 0 to 7
- act_irrep: int32 [96], replicated, may hold values from 0 to 7
Outputs:
- transformed: float32 [9216, 768], P(('grp', 'pair'))
All inputs are finite; a program needn't handle non-finite values.
Results may differ from a plain program's by a relative error of at most 0.0029.
Values sent between devices are 32-bit elements; how exact they have to be, the bound alone decides.
A program may use at most 128 MiB of HBM per device.

v0:
```python
import jax
import jax.numpy as jnp
from jax import lax
from jax.sharding import PartitionSpec as P


def on_device(integrals, coeff, mu_index, nu_index, ao_irrep, act_irrep):
    rows_dev, slab, nbasis = integrals.shape
    nactive = coeff.shape[1]
    groups = lax.axis_size("grp")
    owners = lax.axis_size("pair")
    total = nactive * nactive
    share = total // groups
    subset = share // owners
    all_rows = mu_index.shape[0]
    nsecond = ao_irrep.shape[0]
    slab_coeff = lax.dynamic_slice_in_dim(coeff, lax.axis_index("grp") * slab, slab, 0)
    quarter = jnp.dot(
        integrals.reshape(rows_dev * slab, nbasis), coeff, preferred_element_type=jnp.float32
    )
    quarter = quarter.astype(jnp.bfloat16).reshape(rows_dev, slab, nactive)
    partial_value = jnp.einsum(
        "lp,rlq->rpq", slab_coeff, quarter, preferred_element_type=jnp.float32
    )
    partial_value = partial_value.reshape(rows_dev, total)
    summed = lax.psum(partial_value, "grp")
    mine = lax.dynamic_slice_in_dim(summed, lax.axis_index("grp") * share, share, 1)
    picked = jnp.take(coeff, mu_index, axis=0).astype(jnp.float32)
    onehot = (nu_index[:, None] == jnp.arange(nsecond, dtype=jnp.int32)[None, :]).astype(
        jnp.float32
    )
    amat = (onehot[:, :, None] * picked[:, None, :]).reshape(all_rows, nsecond * nactive)
    sectioned = mine.reshape(rows_dev, owners, subset)
    arrived = lax.all_to_all(sectioned, "pair", split_axis=1, concat_axis=0, tiled=True)
    items = arrived.shape[2]
    flat = arrived.reshape(all_rows, items)
    full = lax.dot_general(flat, amat, (((0,), (0,)), ((), ())), precision=lax.Precision.HIGHEST)
    block_id = lax.axis_index("grp") * owners + lax.axis_index("pair")
    pair_ids = block_id * subset + jnp.arange(subset, dtype=jnp.int32)
    left_irrep = jnp.bitwise_xor(
        jnp.take(act_irrep, pair_ids // nactive), jnp.take(act_irrep, pair_ids % nactive)
    )
    col_ids = jnp.arange(nsecond * nactive, dtype=jnp.int32)
    right_irrep = jnp.bitwise_xor(
        jnp.take(ao_irrep, col_ids // nactive), jnp.take(act_irrep, col_ids % nactive)
    )
    allowed = left_irrep[:, None] == right_irrep[None, :]
    return jnp.where(allowed, full, jnp.zeros_like(full))


def solution(mesh):
    in_specs = (P("pair", "grp", None), P(), P(), P(), P(), P())
    out_specs = P(("grp", "pair"), None)
    return jax.shard_map(
        on_device, mesh=mesh, in_specs=in_specs, out_specs=out_specs, check_vma=False
    )
```

profile of v0, /device:TPU:0, one launch (start us, length us, event | category | flops | bytes accessed | tf_op | source)
XLA Modules:
  0.0 138.6 jit_solution(5353105475166639038)
XLA Ops:
  6.5 0.0 copy-start
  6.5 0.0 all-reduce.2.cloned.1.call-start
  6.5 25.3 %copy.18 = bf16[8,500,2000]{1,0,2:T(8,128)(2,1)} copy(bf16[8,500,2000]{2,0,1:T(8,128)(2,1)} %param.8) | data formatting | bytes 32000000 | tf_op args[0]
  31.8 0.0 copy-start.1
  31.8 36.9 %reshape.187 = bf16[4000,2000]{0,1:T(8,128)(2,1)} reshape(bf16[8,500,2000]{1,0,2:T(8,128)(2,1)} %copy.18) | data formatting | bytes 32000000 | tf_op jit(solution)/shard_map/reshape | solution.py:19
  68.7 0.0 copy-done.1
  68.7 0.0 copy-start.4
  68.7 0.0 copy-start.2
  68.7 0.0 copy-start.3
  68.7 8.4 %convolution_convert_fusion = bf16[4000,96]{0,1:T(8,128)(2,1)S(1)} fusion(bf16[2000,96]{0,1:T(8,128)(2,1)S(1)} %copy-done.1, bf16[4000,2000]{0,1:T(8,128)(2,1)} %reshape.187), kind=kOutput, calls=%fused_computation.4 | convolution fusion | flops 1536384000 | bytes 17152000 | tf_op jit(solution)/shard_map/dot_general | solution.py:18
  77.1 1.7 %reshape.188 = bf16[8,500,96]{1,0,2:T(8,128)(2,1)S(1)} reshape(bf16[4000,96]{0,1:T(8,128)(2,1)S(1)} %convolution_convert_fusion) | data formatting | bytes 1536000 | tf_op jit(solution)/shard_map/reshape | solution.py:21
  78.9 0.5 convolution_bitcast_fusion
  79.4 0.2 copy.20
  79.6 0.9 reshape.189
  80.5 0.0 all-reduce.2.cloned.1.call-update
  80.6 0.3 copy.22
  80.9 0.0 copy-done.4
  80.9 0.0 copy-done.2
  80.9 0.7 fusion.21
  81.7 0.0 copy-done
  81.7 4.8 %gather_fusion = s32[768]{0:T(1024)S(1)} fusion(s32[96]{0:T(128)S(1)} %copy-done, s32[1024]{0:T(1024)S(1)} %pad_clamp_fusion.1), kind=kCustom, calls=%fused_computation.2 | custom fusion | bytes 9216 | tf_op jit(solution)/shard_map/jit(_take)/gather | solution.py:45
  86.5 2.4 %gather_fusion.2 = s32[288]{0:T(512)S(1)} fusion(s32[96]{0:T(128)S(1)} %copy-done, s32[1024]{0:T(1024)S(1)} %pad_clamp_fusion.3), kind=kCustom, calls=%fused_computation.clone | custom fusion | bytes 3456 | tf_op jit(solution)/shard_map/jit(_take)/gather | solution.py:41
  88.9 2.4 %gather_fusion.3 = s32[288]{0:T(512)S(1)} fusion(s32[96]{0:T(128)S(1)} %copy-done, s32[1024]{0:T(1024)S(1)} %pad_clamp_fusion.2), kind=kCustom, calls=%fused_computation.1.clone | custom fusion | bytes 3456 | tf_op jit(solution)/shard_map/jit(_take)/gather | solution.py:41
  91.3 0.0 copy-done.3
  91.3 0.1 fusion.4
  91.3 0.6 gather_fusion.1
  92.0 0.1 select_convert_fusion
  92.1 0.1 broadcast_multiply_fusion
  92.2 0.1 mul.42
  92.3 4.5 %fusion.14 = s32[768]{0:T(1024)S(1)} fusion(s32[]{:T(128)} %bitcast.1, s32[]{:T(128)} %bitcast.2, s32[]{:T(128)} %bitcast.3, s32[]{:T(128)} %bitcast.4, s32[]{:T(128)} %bitcast.5, s32[]{:T(128)} %bitcast.7, s32[]{:T(128)} %bitcast.6), kind=kLoop, calls=%fused_computation.51 | loop fusion | flops 17664 | bytes 3100 | tf_op jit(solution)/shard_map/jit(_take)/gather | solution.py:45
  96.8 0.7 fusion.12
  97.5 18.1 %all-reduce.2.cloned.1.call-done = f32[8,9216]{1,0:T(8,128)} async-done(((f32[8,9216]{1,0:T(8,128)}), f32[8,9216]{1,0:T(8,128)}) %all-reduce.2.cloned.1.call-update) | async-done | bytes 294928 | tf_op jit(solution)/shard_map/psum | solution.py:26
  115.6 0.9 constant_dynamic-slice_fusion
  116.5 0.1 reshape.190
  116.6 0.7 copy.21
  117.3 5.5 %all-to-all-start = ((f32[8,8,288]{2,0,1:T(8,128)}), f32[8,8,288]{2,0,1:T(8,128)S(1)}, u32[]{:S(2)}, u32[]{:S(2)}) async-start(f32[8,8,288]{2,0,1:T(8,128)} %copy.21), calls=%async_computation | async-start | bytes 196608 | tf_op jit(solution)/shard_map/all_to_all | solution.py:34
  122.8 7.1 %all-to-all-done = f32[8,8,288]{2,0,1:T(8,128)S(1)} async-done(((f32[8,8,288]{2,0,1:T(8,128)}), f32[8,8,288]{2,0,1:T(8,128)S(1)}, u32[]{:S(2)}, u32[]{:S(2)}) %all-to-all-start) | async-done | bytes 73760 | tf_op jit(solution)/shard_map/all_to_all | solution.py:34
  129.9 1.8 %convolution_select_fusion = f32[288,768]{1,0:T(8,128)} fusion(f32[64,768]{1,0:T(8,128)S(1)} %mul.42, s32[768]{0:T(1024)S(1)} %fusion.12, s32[288]{0:T(512)S(1)} %select_xor_fusion, f32[8,8,288]{2,0,1:T(8,128)S(1)} %all-to-all-done), kind=kOutput, calls=%fused_computation.5 | convolution fusion | flops 170311680 | bytes 1159296 | tf_op jit(solution)/shard_map/dot_general | solution.py:37
  (10 shorter events, 0.1 us)
Async XLA Ops:
  6.5 75.2 %copy-start = (s32[96]{0:T(128)S(1)}, s32[96]{0:T(128)}, u32[]{:S(2)}) copy-start(s32[96]{0:T(128)} %param.13) | copy-start | bytes 1156
  6.5 109.1 %all-reduce.2.cloned.1.call-start = ((), (), s32[]{:S(2)}) async-start(), calls=%async_computation.1 | async-start | bytes 589824 | tf_op jit(solution)/shard_map/psum | solution.py:26
  31.8 36.9 %copy-start.1 = (bf16[2000,96]{0,1:T(8,128)(2,1)S(1)}, bf16[2000,96]{0,1:T(8,128)(2,1)}, u32[]{:S(2)}) copy-start(bf16[2000,96]{0,1:T(8,128)(2,1)} %param.9) | copy-start | bytes 1152004
  68.7 12.2 %copy-start.4 = (s32[64]{0:T(128)S(1)}, s32[64]{0:T(128)}, u32[]{:S(2)}) copy-start(s32[64]{0:T(128)} %param.10) | copy-start | bytes 772
  68.7 12.3 %copy-start.2 = (s32[8]{0:T(128)S(1)}, s32[8]{0:T(128)}, u32[]{:S(2)}) copy-start(s32[8]{0:T(128)} %param.12) | copy-start | bytes 100
  68.7 22.6 %copy-start.3 = (s32[64]{0:T(128)S(1)}, s32[64]{0:T(128)}, u32[]{:S(2)}) copy-start(s32[64]{0:T(128)} %param.11) | copy-start | bytes 772
  117.3 12.6 %all-to-all-start = ((f32[8,8,288]{2,0,1:T(8,128)}), f32[8,8,288]{2,0,1:T(8,128)S(1)}, u32[]{:S(2)}, u32[]{:S(2)}) async-start(f32[8,8,288]{2,0,1:T(8,128)} %copy.21), calls=%async_computation | async-start | bytes 196608 | tf_op jit(solution)/shard_map/all_to_all | solution.py:34
Sparse Core Ops, SparseCore 0:
  80.7 34.9 all-reduce.1
where the time goes:
time: 140 us; the launch traced here: 139 us
  local copies, waits for them, and re-layouts  77.9 us (56%)
  waiting for transfers between devices  25.2 us (18%)
  between operations  13.6 us (10%)
  matrix products  10.8 us (8%)
  other arithmetic  5.59 us (4%)
  starting transfers between devices  5.51 us (4%)
    reshape x1, local copies, waits for them, and re-layouts, on_device(): integrals.reshape(rows_dev * slab, nbasis)  36.9 us
    unnamed x12, local copies, waits for them, and re-layouts  25.6 us
    psum x1, waiting for transfers between devices, on_device(): summed = lax.psum(partial_value, 'grp')  18.1 us
    dot_general x1, matrix products, on_device(): jnp.dot(integrals.reshape(rows_dev * slab, nbasis), coeff, preferred_elem...  8.4 us
    all_to_all x1, waiting for transfers between devices, on_device(): lax.all_to_all(sectioned, 'pair', split_axis=1, concat_axis=0, tiled=True)  7.11 us
    all_to_all x1, starting transfers between devices, on_device(): lax.all_to_all(sectioned, 'pair', split_axis=1, concat_axis=0, tiled=True)  5.51 us
    gather x1, local copies, waits for them, and re-layouts, on_device(): jnp.take(act_irrep, col_ids % nactive)  4.79 us
    gather x2, other arithmetic, on_device(): jnp.take(ao_irrep, col_ids // nactive)  4.5 us
  transfers between devices with their start and end apart: 2, of which 2 were waited for; matrix products, arithmetic and copies ran while one was open for 12% of the time, Pallas kernels for 0%

commit v1 on v0

v1 whole, which is shorter than its diff:
```python
import functools

import jax
import jax.numpy as jnp
from jax import lax
from jax.experimental import pallas as pl
from jax.experimental.pallas import tpu as pltpu
from jax.sharding import PartitionSpec as P

MESH = pl.DeviceIdType.MESH
F32 = jnp.float32
BF16 = jnp.bfloat16
LANES = 128


def generic(integrals, coeff, mu_index, nu_index, ao_irrep, act_irrep):
    rows_dev, slab, nbasis = integrals.shape
    nactive = coeff.shape[1]
    groups = lax.axis_size("grp")
    owners = lax.axis_size("pair")
    total = nactive * nactive
    share = total // groups
    subset = share // owners
    all_rows = mu_index.shape[0]
    nsecond = ao_irrep.shape[0]
    slab_coeff = lax.dynamic_slice_in_dim(coeff, lax.axis_index("grp") * slab, slab, 0)
    rows_first = integrals.transpose(1, 0, 2).reshape(slab * rows_dev, nbasis)
    quarter = jnp.dot(rows_first, coeff, preferred_element_type=F32)
    quarter = quarter.astype(BF16).reshape(slab, rows_dev, nactive)
    partial_value = jnp.einsum("lp,lrq->rpq", slab_coeff, quarter, preferred_element_type=F32)
    partial_value = partial_value.reshape(rows_dev, total)
    mine = lax.psum_scatter(partial_value, "grp", scatter_dimension=1, tiled=True)
    picked = jnp.take(coeff, mu_index, axis=0).astype(F32)
    onehot = (nu_index[:, None] == jnp.arange(nsecond, dtype=jnp.int32)[None, :]).astype(F32)
    amat = (onehot[:, :, None] * picked[:, None, :]).reshape(all_rows, nsecond * nactive)
    sectioned = mine.reshape(rows_dev, owners, subset)
    arrived = lax.all_to_all(sectioned, "pair", split_axis=1, concat_axis=0, tiled=True)
    flat = arrived.reshape(all_rows, arrived.shape[2])
    full = lax.dot_general(flat, amat, (((0,), (0,)), ((), ())), precision=lax.Precision.HIGHEST)
    block_id = lax.axis_index("grp") * owners + lax.axis_index("pair")
    pair_ids = block_id * subset + jnp.arange(subset, dtype=jnp.int32)
    left_irrep = jnp.bitwise_xor(
        jnp.take(act_irrep, pair_ids // nactive), jnp.take(act_irrep, pair_ids % nactive)
    )
    col_ids = jnp.arange(nsecond * nactive, dtype=jnp.int32)
    right_irrep = jnp.bitwise_xor(
        jnp.take(ao_irrep, col_ids // nactive), jnp.take(act_irrep, col_ids % nactive)
    )
    allowed = left_irrep[:, None] == right_irrep[None, :]
    return jnp.where(allowed, full, jnp.zeros_like(full))


def as_column(row, n):
    eye = lax.broadcasted_iota(jnp.int32, (n, n), 0) == lax.broadcasted_iota(jnp.int32, (n, n), 1)
    return jnp.sum(jnp.where(eye, jnp.broadcast_to(row, (n, n)), 0.0), axis=1, keepdims=True)


def section_of(shape, nactive, nsecond):
    col = lax.broadcasted_iota(jnp.int32, shape, 1)
    section = jnp.zeros(shape, jnp.int32)
    for n in range(1, nsecond):
        section = section + jnp.where(col >= n * nactive, 1, 0)
    return section


def transform_kernel(
    dims, x_hbm, c_hbm, mu_hbm, nu_hbm, ao_hbm, act_hbm, flat_ref, amat_ref, right_ref, actcol_ref,
    xv, cv, cpad, c32, qv, pv, muv, nuv, aov, actv, from_core, kept, from_y, summed, flat,
    x_sem, in_sem, core_send, core_recv, y_send, y_recv, pair_send, pair_recv,
):
    groups, owners, slab, rows_dev, nbasis, nact, nsecond, all_rows, chunk, early = dims
    layers = groups // 2
    per_group = nact // groups
    per_owner = per_group // owners
    grows = per_group * rows_dev
    orows = per_owner * rows_dev
    g = lax.axis_index("grp")
    me = lax.axis_index("pair")
    y, core = g // 2, g % 2
    other = 1 - core
    nchunks = slab * rows_dev // chunk

    small = [
        pltpu.make_async_copy(src, dst, in_sem.at[k])
        for k, (src, dst) in enumerate(
            ((c_hbm, cv), (mu_hbm, muv), (nu_hbm, nuv), (ao_hbm, aov), (act_hbm, actv))
        )
    ]
    small[0].start()

    def x_copy(k):
        where = pl.ds(pl.multiple_of(k * chunk, 16), chunk)
        return pltpu.make_async_copy(x_hbm.at[where, :], xv.at[where, :], x_sem.at[k])

    for k in range(nchunks):
        x_copy(k).start()
    for copy in small[1:]:
        copy.start()

    barrier = pltpu.get_barrier_semaphore()
    pl.semaphore_signal(barrier, inc=1, device_id=(y * 2 + other, me), device_id_type=MESH)
    for d in range(1, layers):
        yy = lax.rem(y + d, layers)
        pl.semaphore_signal(barrier, inc=1, device_id=(yy * 2 + core, me), device_id_type=MESH)
    for d in range(1, owners):
        pl.semaphore_signal(
            barrier, inc=1, device_id=(g, lax.rem(me + d, owners)), device_id_type=MESH
        )

    small[0].wait()
    cpad[...] = jnp.zeros_like(cpad)
    cpad[:, :nact] = cv[...]
    c32[...] = jnp.zeros_like(c32)
    c32[:nbasis, :] = cpad[...].astype(F32)
    span = -(-slab // 256) * 256
    slab_t = c32[pl.ds(g * slab, span), :].T[:nact].astype(BF16)

    def quarter_step(k, carry):
        x_copy(k).wait()
        where = pl.ds(pl.multiple_of(k * chunk, 16), chunk)
        qv[where, :] = jnp.dot(xv[where, :], cpad[...], preferred_element_type=F32)
        return carry

    def half_part(first, count, fresh):
        for i in range(rows_dev):
            q = qv[pl.ds(first * rows_dev + i, count, stride=rows_dev), :].astype(BF16)
            part = jnp.dot(slab_t[:, first : first + count], q, preferred_element_type=F32)
            spot = pl.ds(i, nact, stride=rows_dev)
            pv[spot, :] = part if fresh else pv[spot, :] + part

    lax.fori_loop(0, early, quarter_step, 0)
    cut = early * chunk // rows_dev // 256 * 256
    if cut:
        half_part(0, cut, True)
    lax.fori_loop(early, nchunks, quarter_step, 0)
    half_part(cut, slab - cut, not cut)

    pl.semaphore_wait(barrier, layers + owners - 1)

    steps = owners // 2
    srows = 2 * orows

    def spot_of(step):
        b = lax.rem(me // 2 + steps // 2 + step, steps)
        return b, pl.multiple_of(b * srows, 8)

    def core_copy(d, step):
        layer = lax.rem(y + d, layers)
        _, at = spot_of(step)
        src = pl.multiple_of((layer * 2 + other) * grows + at, 8)
        return pltpu.make_async_remote_copy(
            src_ref=pv.at[pl.ds(src, srows), :],
            dst_ref=from_core.at[d, pl.ds(at, srows), :],
            send_sem=core_send.at[d, step],
            recv_sem=core_recv.at[d, step],
            device_id=(y * 2 + other, me),
            device_id_type=MESH,
        )

    def y_copy(d, step):
        layer = lax.rem(y + d, layers)
        _, at = spot_of(step)
        return pltpu.make_async_remote_copy(
            src_ref=kept.at[d, pl.ds(at, srows), :],
            dst_ref=from_y.at[d - 1, pl.ds(at, srows), :],
            send_sem=y_send.at[d - 1, step],
            recv_sem=y_recv.at[d - 1, step],
            device_id=(layer * 2 + core, me),
            device_id_type=MESH,
        )

    def pair_copy(d):
        to = lax.rem(me + d, owners)
        return pltpu.make_async_remote_copy(
            src_ref=summed.at[pl.ds(pl.multiple_of(to * orows, 8), orows), :],
            dst_ref=flat.at[pl.ds(pl.multiple_of(me * orows, 8), orows), :],
            send_sem=pair_send.at[d],
            recv_sem=pair_recv.at[d],
            device_id=(g, to),
            device_id_type=MESH,
        )

    order = list(range(1, layers)) + [0]
    for d in order:
        for step in range(steps):
            core_copy(d, step).start()
    for d in order:
        for step in range(steps):
            core_copy(d, step).wait_recv()
            _, at = spot_of(step)
            layer = lax.rem(y + d, layers)
            src = pl.multiple_of((layer * 2 + core) * grows + at, 8)
            here = pl.ds(at, srows)
            kept[d, here, :] = pv[pl.ds(src, srows), :] + from_core[d, here, :]
            if d:
                y_copy(d, step).start()

    for copy in small[1:]:
        copy.wait()
    cols = nsecond * nact
    mu_col = as_column(muv[...].astype(F32), all_rows)
    nu_col = as_column(nuv[...].astype(F32), all_rows)
    basis = lax.broadcasted_iota(jnp.int32, (all_rows, nbasis), 1).astype(F32)
    pick = jnp.where(basis == mu_col, 1.0, 0.0).astype(BF16)
    picked = jnp.dot(pick, cv[...], preferred_element_type=F32).astype(BF16)
    section = section_of((nact, cols), nact, nsecond)
    inside = lax.broadcasted_iota(jnp.int32, (nact, cols), 1) - section * nact
    spread = jnp.where(
        inside == lax.broadcasted_iota(jnp.int32, (nact, cols), 0), 1.0, 0.0
    ).astype(BF16)
    wide = jnp.dot(picked, spread, preferred_element_type=F32)
    nu_of_col = section_of((all_rows, cols), nact, nsecond).astype(F32)
    amat_ref[...] = jnp.where(nu_of_col == nu_col, wide, 0.0).astype(BF16)
    act_row = actv[...].astype(F32)
    act_wide = jnp.dot(
        jnp.broadcast_to(act_row, (8, nact)).astype(BF16), spread, preferred_element_type=F32
    )
    sec8 = section_of((8, cols), nact, nsecond)
    ao_sel = jnp.where(
        lax.broadcasted_iota(jnp.int32, (nsecond, cols), 0)
        == section_of((nsecond, cols), nact, nsecond),
        1.0,
        0.0,
    ).astype(BF16)
    ao_wide = jnp.dot(
        jnp.broadcast_to(aov[...].astype(F32), (8, nsecond)).astype(BF16),
        ao_sel,
        preferred_element_type=F32,
    )
    del sec8
    right_ref[...] = jnp.bitwise_xor(act_wide.astype(jnp.int32), ao_wide.astype(jnp.int32))
    actcol_ref[...] = jnp.broadcast_to(as_column(act_row, nact), (nact, LANES)).astype(jnp.int32)

    for step in range(steps):
        b, at = spot_of(step)
        here = pl.ds(at, srows)
        total = kept[0, here, :]
        for d in range(1, layers):
            y_copy(d, step).wait_recv()
            total = total + from_y[d - 1, here, :]
        summed[here, :] = total
        for half in range(2):
            to = b * 2 + half

            @pl.when(to != me)
            def _():
                gap = lax.rem(to - me + owners, owners)
                pair_copy(gap).start()

    own = pl.ds(pl.multiple_of(me * orows, 8), orows)
    flat[own, :] = summed[own, :]
    for d in range(1, owners):
        pair_copy(d).wait_recv()
    flat_ref[...] = flat[...]
    for d in order:
        for step in range(steps):
            core_copy(d, step).wait_send()
            if d:
                y_copy(d, step).wait_send()
    for d in range(1, owners):
        pair_copy(d).wait_send()


def finish_kernel(dims, act_ref, flat_ref, amat_ref, right_ref, actcol_ref, out_ref):
    owners, rows_dev, per_owner, nact, cols = dims
    block = lax.axis_index("grp") * owners + lax.axis_index("pair")
    a = amat_ref[...]
    weights = jnp.concatenate([a, a, a], axis=0)
    right = right_ref[:1, :]
    act_col = actcol_ref[:, :1]
    for j in range(per_owner):
        f = jnp.concatenate(
            [
                flat_ref[pl.ds((s * per_owner + j) * rows_dev, rows_dev), :]
                for s in range(owners)
            ],
            axis=0,
        )
        high = f.astype(BF16)
        rest = f - high.astype(F32)
        mid = rest.astype(BF16)
        low = (rest - mid.astype(F32)).astype(BF16)
        parts = jnp.concatenate([high, mid, low], axis=0).astype(F32).T[:nact].astype(BF16)
        full = jnp.dot(parts, weights, preferred_element_type=F32)
        left = jnp.bitwise_xor(act_col, act_ref[block * per_owner + j])
        out_ref[pl.ds(j * nact, nact), :] = jnp.where(left == right, full, 0.0)


def fast(integrals, coeff, mu_index, nu_index, ao_irrep, act_irrep):
    rows_dev, slab, nbasis = integrals.shape
    nact = coeff.shape[1]
    groups, owners = lax.axis_size("grp"), lax.axis_size("pair")
    all_rows, nsecond = mu_index.shape[0], ao_irrep.shape[0]
    layers = groups // 2
    per_owner = nact // groups // owners
    grows = nact // groups * rows_dev
    cols = nsecond * nact
    rows = slab * rows_dev
    chunk = max(c for c in range(16, 513, 16) if rows % c == 0)
    nchunks = rows // chunk
    early = min(nchunks, -(-256 * rows_dev // chunk))
    dims = (groups, owners, slab, rows_dev, nbasis, nact, nsecond, all_rows, chunk, early)
    span = -(-slab // 256) * 256
    x = integrals.transpose(1, 0, 2).reshape(rows, nbasis)
    steps = owners // 2
    any_spec = pl.BlockSpec(memory_space=pl.ANY)
    vmem = pl.BlockSpec(memory_space=pltpu.VMEM)
    flat, amat, right, actcol = pl.pallas_call(
        functools.partial(transform_kernel, dims),
        out_shape=(
            jax.ShapeDtypeStruct((grows, LANES), F32),
            jax.ShapeDtypeStruct((all_rows, cols), BF16),
            jax.ShapeDtypeStruct((8, cols), jnp.int32),
            jax.ShapeDtypeStruct((nact, LANES), jnp.int32),
        ),
        in_specs=[any_spec] * 6,
        out_specs=(vmem,) * 4,
        scratch_shapes=[
            pltpu.VMEM((rows, nbasis), BF16),
            pltpu.VMEM((nbasis, nact), BF16),
            pltpu.VMEM((nbasis, LANES), BF16),
            pltpu.VMEM((slab * (groups - 1) + span + 8, LANES), F32),
            pltpu.VMEM((rows, LANES), F32),
            pltpu.VMEM((nact * rows_dev, LANES), F32),
            pltpu.VMEM((1, all_rows), jnp.int32),
            pltpu.VMEM((1, all_rows), jnp.int32),
            pltpu.VMEM((1, nsecond), jnp.int32),
            pltpu.VMEM((1, nact), jnp.int32),
            pltpu.VMEM((layers, grows, LANES), F32),
            pltpu.VMEM((layers, grows, LANES), F32),
            pltpu.VMEM((layers - 1, grows, LANES), F32),
            pltpu.VMEM((grows, LANES), F32),
            pltpu.VMEM((grows, LANES), F32),
            pltpu.SemaphoreType.DMA((nchunks,)),
            pltpu.SemaphoreType.DMA((5,)),
            pltpu.SemaphoreType.DMA((layers, steps)),
            pltpu.SemaphoreType.DMA((layers, steps)),
            pltpu.SemaphoreType.DMA((layers - 1, steps)),
            pltpu.SemaphoreType.DMA((layers - 1, steps)),
            pltpu.SemaphoreType.DMA((owners,)),
            pltpu.SemaphoreType.DMA((owners,)),
        ],
        compiler_params=pltpu.CompilerParams(
            collective_id=0, has_side_effects=True, vmem_limit_bytes=48 * 1024 * 1024
        ),
        cost_estimate=pl.CostEstimate(
            flops=2 * rows * nbasis * nact, bytes_accessed=rows * nbasis * 2, transcendentals=0
        ),
    )(
        x, coeff, mu_index.reshape(1, -1), nu_index.reshape(1, -1),
        ao_irrep.reshape(1, -1), act_irrep.reshape(1, -1),
    )
    return pl.pallas_call(
        functools.partial(finish_kernel, (owners, rows_dev, per_owner, nact, cols)),
        out_shape=jax.ShapeDtypeStruct((per_owner * nact, cols), F32),
        in_specs=[pl.BlockSpec(memory_space=pltpu.SMEM)] + [vmem] * 4,
        out_specs=vmem,
        compiler_params=pltpu.CompilerParams(vmem_limit_bytes=32 * 1024 * 1024),
    )(act_irrep, flat, amat, right, actcol)


def on_device(integrals, coeff, mu_index, nu_index, ao_irrep, act_irrep):
    rows_dev, slab, _ = integrals.shape
    nact = coeff.shape[1]
    groups, owners = lax.axis_size("grp"), lax.axis_size("pair")
    whole_rows = nact % (groups * owners) == 0
    fits = rows_dev == 8 and groups % 2 == 0 and groups > 2 and owners % 2 == 0
    if whole_rows and fits and slab * rows_dev % 16 == 0 and nact <= LANES:
        return fast(integrals, coeff, mu_index, nu_index, ao_irrep, act_irrep)
    return generic(integrals, coeff, mu_index, nu_index, ao_irrep, act_irrep)


def solution(mesh):
    in_specs = (P("pair", "grp", None), P(), P(), P(), P(), P())
    out_specs = P(("grp", "pair"), None)
    return jax.shard_map(
        on_device, mesh=mesh, in_specs=in_specs, out_specs=out_specs, check_vma=False
    )
```

time: 140 us -> 28.1 us (0.20)
  local copies, waits for them, and re-layouts: 77.9 us -> 3.91 us
  waiting for transfers between devices: 25.2 us -> 0 us
  Pallas kernels: 0 us -> 24 us
  between operations: 13.6 us -> 0.02 us
  matrix products: 10.8 us -> 0 us
  other arithmetic: 5.59 us -> 0 us
  starting transfers between devices: 5.51 us -> 0 us
    reshape x5 -> x0, local copies, waits for them, and re-layouts: 40.3 us -> none  [the longest x1 36.9 us: on_device(): integrals.reshape(rows_dev * slab, nbasis)]
    pallas_call x0 -> x2, Pallas kernels: none -> 24 us  [the longest x1 22.2 us: fast(): pl.pallas_call(functools.partial(transform_kernel, dims), out_shape=(jax....]
    unnamed x12 -> x9, local copies, waits for them, and re-layouts: 25.6 us -> 3.91 us
    psum x1 -> x0, waiting for transfers between devices: 18.1 us -> none  [on_device(): summed = lax.psum(partial_value, 'grp')]
    gather x5 -> x0, local copies, waits for them, and re-layouts: 10.8 us -> none  [the longest x1 4.79 us: on_device(): jnp.take(act_irrep, col_ids % nactive)]
    dot_general x3 -> x0, matrix products: 10.8 us -> none  [the longest x1 8.4 us: on_device(): jnp.dot(integrals.reshape(rows_dev * slab, nbasis), coeff, preferred_elem...]
    all_to_all x1 -> x0, waiting for transfers between devices: 7.11 us -> none  [on_device(): lax.all_to_all(sectioned, 'pair', split_axis=1, concat_axis=0, tiled=True)]
    all_to_all x1 -> x0, starting transfers between devices: 5.51 us -> none  [on_device(): lax.all_to_all(sectioned, 'pair', split_axis=1, concat_axis=0, tiled=True)]
  transfers between devices with their start and end apart: 2 -> 0, of which waited for: 2 -> 0; matrix products, arithmetic and copies ran while one was open for 12% -> 0% of each run, Pallas kernels for 0% -> 0%
where the time goes in v1:
time: 28.1 us; the launch traced here: 27.9 us
  Pallas kernels  24 us (85%)
  local copies, waits for them, and re-layouts  3.91 us (14%)
    pallas_call x1, Pallas kernels, fast(): pl.pallas_call(functools.partial(transform_kernel, dims), out_shape=(jax....  22.2 us
    unnamed x9, local copies, waits for them, and re-layouts  3.91 us
    pallas_call x1, Pallas kernels, fast(): pl.pallas_call(functools.partial(finish_kernel, (owners, rows_dev, per_ow...  1.79 us

profile of v1, /device:TPU:0, one launch (start us, length us, event | category | flops | bytes accessed | tf_op | source)
XLA Modules:
  0.0 27.9 jit_solution(11313305796478415592)
XLA Ops:
  0.0 1.3 %copy.7.c_hbm = bf16[2000,96]{1,0:T(8,128)(2,1)S(1)} copy(bf16[2000,96]{0,1:T(8,128)(2,1)} %param.7) | data formatting | bytes 768000 | tf_op args[1]
  1.3 0.0 copy-start
  1.3 0.7 %copy-done = s32[96]{0:T(128)S(1)} copy-done((s32[96]{0:T(128)S(1)}, s32[96]{0:T(128)}, u32[]{:S(2)}) %copy-start) | copy-done | bytes 408
  2.0 0.0 copy-start.1
  2.0 0.7 %copy-done.1 = s32[64]{0:T(128)S(1)} copy-done((s32[64]{0:T(128)S(1)}, s32[64]{0:T(128)}, u32[]{:S(2)}) %copy-start.1) | copy-done | bytes 280
  2.6 0.0 copy-start.2
  2.6 0.7 %copy-done.2 = s32[64]{0:T(128)S(1)} copy-done((s32[64]{0:T(128)S(1)}, s32[64]{0:T(128)}, u32[]{:S(2)}) %copy-start.2) | copy-done | bytes 280
  3.3 0.0 copy-start.3
  3.3 0.7 %copy-done.3 = s32[8]{0:T(128)S(1)} copy-done((s32[8]{0:T(128)S(1)}, s32[8]{0:T(128)}, u32[]{:S(2)}) %copy-start.3) | copy-done | bytes 56
  3.9 22.2 %shard_map.64 = (f32[192,128]{1,0:T(8,128)S(1)}, bf16[64,768]{1,0:T(8,128)(2,1)S(1)}, s32[8,768]{1,0:T(8,128)S(1)}, s32[96,128]{1,0:T(8,128)S(1)}) custom-call(bf16[4000,2000]{1,0:T(8,128)(2,1)} %bitcast.11, bf16[2000,96]{1,0:T(8,128)(2,1)S(1)} %copy.7.c_hbm, s32[1,64]{1,0:T(1,128)S(1)} %bitcast.8, s32[1,64]{1,0:T(1,128)S(1)} %bitcast.9, ...), custom_call_target="tpu_custom_call" | custom-call | flops 1536000000 | bytes 16000000 | tf_op jit(solution)/shard_map/pallas_call | solution.py:308
  26.1 1.8 %shard_map.65 = f32[288,768]{1,0:T(8,128)} custom-call(s32[96]{0:T(128)S(1)} %copy-done, f32[192,128]{1,0:T(8,128)S(1)} %get-tuple-element.9.flat_ref, bf16[64,768]{1,0:T(8,128)(2,1)S(1)} %get-tuple-element.10.amat_ref, s32[8,768]{1,0:T(8,128)S(1)} %get-tuple-element.11.right_ref, s32[96,128]{1,0:T(8,128)S(1)} %get-tuple-element.12.actcol_ref), custom_call_target="tpu_custom_call" | custom-call | tf_op jit(solution)/shard_map/pallas_call | solution.py:353
Async XLA Ops:
  1.3 0.7 %copy-start = (s32[96]{0:T(128)S(1)}, s32[96]{0:T(128)}, u32[]{:S(2)}) copy-start(s32[96]{0:T(128)} %act_ref.1) | copy-start | bytes 1156
  2.0 0.7 %copy-start.1 = (s32[64]{0:T(128)S(1)}, s32[64]{0:T(128)}, u32[]{:S(2)}) copy-start(s32[64]{0:T(128)} %param.8) | copy-start | bytes 772
  2.6 0.7 %copy-start.2 = (s32[64]{0:T(128)S(1)}, s32[64]{0:T(128)}, u32[]{:S(2)}) copy-start(s32[64]{0:T(128)} %param.9) | copy-start | bytes 772
  3.3 0.7 %copy-start.3 = (s32[8]{0:T(128)S(1)}, s32[8]{0:T(128)}, u32[]{:S(2)}) copy-start(s32[8]{0:T(128)} %param.10) | copy-start | bytes 100

commit v2 on v1

--- a/solution.py
+++ b/solution.py
@@ -11,6 +11,7 @@
 F32 = jnp.float32
 BF16 = jnp.bfloat16
 LANES = 128
+VMEM_LIMIT = 64 * 1024 * 1024
 
 
 def generic(integrals, coeff, mu_index, nu_index, ao_irrep, act_irrep):
@@ -50,11 +51,6 @@
     return jnp.where(allowed, full, jnp.zeros_like(full))
 
 
-def as_column(row, n):
-    eye = lax.broadcasted_iota(jnp.int32, (n, n), 0) == lax.broadcasted_iota(jnp.int32, (n, n), 1)
-    return jnp.sum(jnp.where(eye, jnp.broadcast_to(row, (n, n)), 0.0), axis=1, keepdims=True)
-
-
 def section_of(shape, nactive, nsecond):
     col = lax.broadcasted_iota(jnp.int32, shape, 1)
     section = jnp.zeros(shape, jnp.int32)
@@ -64,9 +60,9 @@
 
 
 def transform_kernel(
-    dims, x_hbm, c_hbm, mu_hbm, nu_hbm, ao_hbm, act_hbm, flat_ref, amat_ref, right_ref, actcol_ref,
-    xv, cv, cpad, c32, qv, pv, muv, nuv, aov, actv, from_core, kept, from_y, summed, flat,
-    x_sem, in_sem, core_send, core_recv, y_send, y_recv, pair_send, pair_recv,
+    dims, x_hbm, c_hbm, mu_hbm, nu_hbm, ao_hbm, act_hbm, out_hbm,
+    xv, cv, ct, cpad, c32, qv, pv, muv, nuv, aov, actv, from_core, kept, from_y, summed, flat,
+    picked, nu_col, act_col, out, out_sem, x_sem, in_sem, core_send, core_recv, y_send, y_recv, pair_send, pair_recv,
 ):
     groups, owners, slab, rows_dev, nbasis, nact, nsecond, all_rows, chunk, early = dims
     layers = groups // 2
@@ -108,12 +104,10 @@
         )
 
     small[0].wait()
-    cpad[...] = jnp.zeros_like(cpad)
-    cpad[:, :nact] = cv[...]
-    c32[...] = jnp.zeros_like(c32)
-    c32[:nbasis, :] = cpad[...].astype(F32)
-    span = -(-slab // 256) * 256
-    slab_t = c32[pl.ds(g * slab, span), :].T[:nact].astype(BF16)
+    ct[...] = jnp.zeros_like(ct)
+    ct[:nact, :nbasis] = cv[...].astype(F32)
+    c32[...] = ct[...].T
+    cpad[...] = c32[:nbasis, :].astype(BF16)
 
     def quarter_step(k, carry):
         x_copy(k).wait()
@@ -122,13 +116,23 @@
         return carry
 
     def half_part(first, count, fresh):
-        for i in range(rows_dev):
-            q = qv[pl.ds(first * rows_dev + i, count, stride=rows_dev), :].astype(BF16)
+        for i in range(0, rows_dev, 2):
+            q = jnp.concatenate(
+                [
+                    qv[pl.ds(first * rows_dev + i + k, count, stride=rows_dev), :].astype(BF16)
+                    for k in range(2)
+                ],
+                axis=1,
+            )
             part = jnp.dot(slab_t[:, first : first + count], q, preferred_element_type=F32)
-            spot = pl.ds(i, nact, stride=rows_dev)
-            pv[spot, :] = part if fresh else pv[spot, :] + part
+            for k in range(2):
+                spot = pl.ds(i + k, nact, stride=rows_dev)
+                mine = part[:, k * LANES : (k + 1) * LANES]
+                pv[spot, :] = mine if fresh else pv[spot, :] + mine
 
     lax.fori_loop(0, early, quarter_step, 0)
+    span = -(-slab // 256) * 256
+    slab_t = c32[pl.ds(g * slab, span), :].T[:nact].astype(BF16)
     cut = early * chunk // rows_dev // 256 * 256
     if cut:
         half_part(0, cut, True)
@@ -195,42 +199,6 @@
             if d:
                 y_copy(d, step).start()
 
-    for copy in small[1:]:
-        copy.wait()
-    cols = nsecond * nact
-    mu_col = as_column(muv[...].astype(F32), all_rows)
-    nu_col = as_column(nuv[...].astype(F32), all_rows)
-    basis = lax.broadcasted_iota(jnp.int32, (all_rows, nbasis), 1).astype(F32)
-    pick = jnp.where(basis == mu_col, 1.0, 0.0).astype(BF16)
-    picked = jnp.dot(pick, cv[...], preferred_element_type=F32).astype(BF16)
-    section = section_of((nact, cols), nact, nsecond)
-    inside = lax.broadcasted_iota(jnp.int32, (nact, cols), 1) - section * nact
-    spread = jnp.where(
-        inside == lax.broadcasted_iota(jnp.int32, (nact, cols), 0), 1.0, 0.0
-    ).astype(BF16)
-    wide = jnp.dot(picked, spread, preferred_element_type=F32)
-    nu_of_col = section_of((all_rows, cols), nact, nsecond).astype(F32)
-    amat_ref[...] = jnp.where(nu_of_col == nu_col, wide, 0.0).astype(BF16)
-    act_row = actv[...].astype(F32)
-    act_wide = jnp.dot(
-        jnp.broadcast_to(act_row, (8, nact)).astype(BF16), spread, preferred_element_type=F32
-    )
-    sec8 = section_of((8, cols), nact, nsecond)
-    ao_sel = jnp.where(
-        lax.broadcasted_iota(jnp.int32, (nsecond, cols), 0)
-        == section_of((nsecond, cols), nact, nsecond),
-        1.0,
-        0.0,
-    ).astype(BF16)
-    ao_wide = jnp.dot(
-        jnp.broadcast_to(aov[...].astype(F32), (8, nsecond)).astype(BF16),
-        ao_sel,
-        preferred_element_type=F32,
-    )
-    del sec8
-    right_ref[...] = jnp.bitwise_xor(act_wide.astype(jnp.int32), ao_wide.astype(jnp.int32))
-    actcol_ref[...] = jnp.broadcast_to(as_column(act_row, nact), (nact, LANES)).astype(jnp.int32)
-
     for step in range(steps):
         b, at = spot_of(step)
         here = pl.ds(at, srows)
@@ -249,9 +217,62 @@
 
     own = pl.ds(pl.multiple_of(me * orows, 8), orows)
     flat[own, :] = summed[own, :]
+    for copy in small[1:]:
+        copy.wait()
+    cols = nsecond * nact
+
+    def pick_row(i, carry):
+        picked[pl.ds(i, 1), :] = c32[pl.ds(muv[i], 1), :]
+        nu_col[pl.ds(i, 1), :] = jnp.broadcast_to(nuv[i], (1, LANES))
+        return carry
+
+    def act_row(i, carry):
+        act_col[pl.ds(i, 1), :] = jnp.broadcast_to(actv[i], (1, LANES))
+        return carry
+
+    lax.fori_loop(0, all_rows, pick_row, 0)
+    lax.fori_loop(0, nact, act_row, 0)
+    section = section_of((1, cols), nact, nsecond)
+    inside = lax.broadcasted_iota(jnp.int32, (1, cols), 1) - section * nact
+    spread = inside == lax.broadcasted_iota(jnp.int32, (nact, cols), 0)
+    wide = jnp.dot(
+        picked[:, :nact].astype(BF16),
+        jnp.where(spread, 1.0, 0.0).astype(BF16),
+        preferred_element_type=F32,
+    )
+    amat = jnp.where(section == nu_col[:, :1], wide, 0.0).astype(BF16)
+    weights = jnp.concatenate([amat, amat, amat], axis=0)
+    act_wide = jnp.sum(
+        jnp.where(spread, act_col[:, :1].astype(F32), 0.0), axis=0, keepdims=True
+    ).astype(jnp.int32)
+    ao_wide = jnp.zeros((1, cols), jnp.int32)
+    for n in range(nsecond):
+        ao_wide = jnp.where(section == n, aov[n], ao_wide)
+    right = jnp.bitwise_xor(act_wide, ao_wide)
+
     for d in range(1, owners):
         pair_copy(d).wait_recv()
-    flat_ref[...] = flat[...]
+    copies = []
+    for j in range(per_owner):
+        f = jnp.concatenate(
+            [
+                flat[pl.ds((s * per_owner + j) * rows_dev, rows_dev), :]
+                for s in range(owners)
+            ],
+            axis=0,
+        )
+        high = f.astype(BF16)
+        rest = f - high.astype(F32)
+        mid = rest.astype(BF16)
+        low = (rest - mid.astype(F32)).astype(BF16)
+        parts = jnp.concatenate([high, mid, low], axis=0).astype(F32).T[:nact].astype(BF16)
+        full = jnp.dot(parts, weights, preferred_element_type=F32)
+        p = (g * owners + me) * per_owner + j
+        left = jnp.bitwise_xor(act_col[:, :1], act_col[pl.ds(p, 1), :1])
+        here = pl.ds(j * nact, nact)
+        out[here, :] = jnp.where(left == right, full, 0.0)
+        copies.append(pltpu.make_async_copy(out.at[here, :], out_hbm.at[here, :], out_sem.at[j]))
+        copies[-1].start()
     for d in order:
         for step in range(steps):
             core_copy(d, step).wait_send()
@@ -259,31 +280,8 @@
                 y_copy(d, step).wait_send()
     for d in range(1, owners):
         pair_copy(d).wait_send()
-
-
-def finish_kernel(dims, act_ref, flat_ref, amat_ref, right_ref, actcol_ref, out_ref):
-    owners, rows_dev, per_owner, nact, cols = dims
-    block = lax.axis_index("grp") * owners + lax.axis_index("pair")
-    a = amat_ref[...]
-    weights = jnp.concatenate([a, a, a], axis=0)
-    right = right_ref[:1, :]
-    act_col = actcol_ref[:, :1]
-    for j in range(per_owner):
-        f = jnp.concatenate(
-            [
-                flat_ref[pl.ds((s * per_owner + j) * rows_dev, rows_dev), :]
-                for s in range(owners)
-            ],
-            axis=0,
-        )
-        high = f.astype(BF16)
-        rest = f - high.astype(F32)
-        mid = rest.astype(BF16)
-        low = (rest - mid.astype(F32)).astype(BF16)
-        parts = jnp.concatenate([high, mid, low], axis=0).astype(F32).T[:nact].astype(BF16)
-        full = jnp.dot(parts, weights, preferred_element_type=F32)
-        left = jnp.bitwise_xor(act_col, act_ref[block * per_owner + j])
-        out_ref[pl.ds(j * nact, nact), :] = jnp.where(left == right, full, 0.0)
+    for copy in copies:
+        copy.wait()
 
 
 def fast(integrals, coeff, mu_index, nu_index, ao_irrep, act_irrep):
@@ -301,36 +299,37 @@
     early = min(nchunks, -(-256 * rows_dev // chunk))
     dims = (groups, owners, slab, rows_dev, nbasis, nact, nsecond, all_rows, chunk, early)
     span = -(-slab // 256) * 256
+    deep = -(-(slab * (groups - 1) + span) // LANES) * LANES
     x = integrals.transpose(1, 0, 2).reshape(rows, nbasis)
     steps = owners // 2
-    any_spec = pl.BlockSpec(memory_space=pl.ANY)
-    vmem = pl.BlockSpec(memory_space=pltpu.VMEM)
-    flat, amat, right, actcol = pl.pallas_call(
+    hbm = pl.BlockSpec(memory_space=pltpu.HBM)
+    return pl.pallas_call(
         functools.partial(transform_kernel, dims),
-        out_shape=(
-            jax.ShapeDtypeStruct((grows, LANES), F32),
-            jax.ShapeDtypeStruct((all_rows, cols), BF16),
-            jax.ShapeDtypeStruct((8, cols), jnp.int32),
-            jax.ShapeDtypeStruct((nact, LANES), jnp.int32),
-        ),
-        in_specs=[any_spec] * 6,
-        out_specs=(vmem,) * 4,
+        out_shape=jax.ShapeDtypeStruct((per_owner * nact, cols), F32),
+        in_specs=[hbm] * 6,
+        out_specs=hbm,
         scratch_shapes=[
             pltpu.VMEM((rows, nbasis), BF16),
-            pltpu.VMEM((nbasis, nact), BF16),
+            pltpu.VMEM((nact, nbasis), BF16),
+            pltpu.VMEM((LANES, deep), F32),
             pltpu.VMEM((nbasis, LANES), BF16),
-            pltpu.VMEM((slab * (groups - 1) + span + 8, LANES), F32),
+            pltpu.VMEM((deep, LANES), F32),
             pltpu.VMEM((rows, LANES), F32),
             pltpu.VMEM((nact * rows_dev, LANES), F32),
-            pltpu.VMEM((1, all_rows), jnp.int32),
-            pltpu.VMEM((1, all_rows), jnp.int32),
-            pltpu.VMEM((1, nsecond), jnp.int32),
-            pltpu.VMEM((1, nact), jnp.int32),
+            pltpu.SMEM((all_rows,), jnp.int32),
+            pltpu.SMEM((all_rows,), jnp.int32),
+            pltpu.SMEM((nsecond,), jnp.int32),
+            pltpu.SMEM((nact,), jnp.int32),
             pltpu.VMEM((layers, grows, LANES), F32),
             pltpu.VMEM((layers, grows, LANES), F32),
             pltpu.VMEM((layers - 1, grows, LANES), F32),
             pltpu.VMEM((grows, LANES), F32),
             pltpu.VMEM((grows, LANES), F32),
+            pltpu.VMEM((all_rows, LANES), F32),
+            pltpu.VMEM((all_rows, LANES), jnp.int32),
+            pltpu.VMEM((nact, LANES), jnp.int32),
+            pltpu.VMEM((per_owner * nact, cols), F32),
+            pltpu.SemaphoreType.DMA((per_owner,)),
             pltpu.SemaphoreType.DMA((nchunks,)),
             pltpu.SemaphoreType.DMA((5,)),
             pltpu.SemaphoreType.DMA((layers, steps)),
@@ -341,22 +340,12 @@
             pltpu.SemaphoreType.DMA((owners,)),
         ],
         compiler_params=pltpu.CompilerParams(
-            collective_id=0, has_side_effects=True, vmem_limit_bytes=48 * 1024 * 1024
+            collective_id=0, has_side_effects=True, vmem_limit_bytes=VMEM_LIMIT
         ),
         cost_estimate=pl.CostEstimate(
             flops=2 * rows * nbasis * nact, bytes_accessed=rows * nbasis * 2, transcendentals=0
         ),
-    )(
-        x, coeff, mu_index.reshape(1, -1), nu_index.reshape(1, -1),
-        ao_irrep.reshape(1, -1), act_irrep.reshape(1, -1),
-    )
-    return pl.pallas_call(
-        functools.partial(finish_kernel, (owners, rows_dev, per_owner, nact, cols)),
-        out_shape=jax.ShapeDtypeStruct((per_owner * nact, cols), F32),
-        in_specs=[pl.BlockSpec(memory_space=pltpu.SMEM)] + [vmem] * 4,
-        out_specs=vmem,
-        compiler_params=pltpu.CompilerParams(vmem_limit_bytes=32 * 1024 * 1024),
-    )(act_irrep, flat, amat, right, actcol)
+    )(x, coeff.T, mu_index, nu_index, ao_irrep, act_irrep)
 
 
 def on_device(integrals, coeff, mu_index, nu_index, ao_irrep, act_irrep):

time: 28.1 us -> 27.6 us (0.982)
  local copies, waits for them, and re-layouts: 3.91 us -> 2.14 us
  Pallas kernels: 24 us -> 25.3 us
    unnamed x9 -> x1, local copies, waits for them, and re-layouts: 3.91 us -> 2.14 us
    pallas_call x2 -> x1, Pallas kernels: 24 us -> 25.3 us  [fast(): pl.pallas_call(functools.partial(transform_kernel, dims), out_shape=jax.S...]
where the time goes in v2:
time: 27.6 us; the launch traced here: 27.5 us
  Pallas kernels  25.3 us (92%)
  local copies, waits for them, and re-layouts  2.14 us (8%)
    pallas_call x1, Pallas kernels, fast(): pl.pallas_call(functools.partial(transform_kernel, dims), out_shape=jax.S...  25.3 us
    unnamed x1, local copies, waits for them, and re-layouts  2.14 us

profile of v2, /device:TPU:0, one launch (start us, length us, event | category | flops | bytes accessed | tf_op | source)
XLA Modules:
  0.0 27.5 jit_solution(12108099450205090324)
XLA Ops:
  0.0 25.3 %shard_map.64 = f32[288,768]{1,0:T(8,128)} custom-call(bf16[4000,2000]{1,0:T(8,128)(2,1)} %bitcast.4, bf16[96,2000]{1,0:T(8,128)(2,1)} %bitcast.5, s32[64]{0:T(128)} %mu_hbm.1, s32[64]{0:T(128)} %nu_hbm.1, s32[8]{0:T(128)} %ao_hbm.1, s32[96]{0:T(128)} %act_hbm.1), custom_call_target="tpu_custom_call" | custom-call | flops 1536000000 | bytes 16000000 | tf_op jit(solution)/shard_map/pallas_call | solution.py:306
  25.3 2.1 %copy.8 = f32[288,768]{1,0:T(8,128)} copy(f32[288,768]{1,0:T(8,128)} %shard_map.64) | data formatting | bytes 1769472

commit v3 on v2

--- a/solution.py
+++ b/solution.py
@@ -60,9 +60,9 @@
 
 
 def transform_kernel(
-    dims, x_hbm, c_hbm, mu_hbm, nu_hbm, ao_hbm, act_hbm, out_hbm,
-    xv, cv, ct, cpad, c32, qv, pv, muv, nuv, aov, actv, from_core, kept, from_y, summed, flat,
-    picked, nu_col, act_col, out, out_sem, x_sem, in_sem, core_send, core_recv, y_send, y_recv, pair_send, pair_recv,
+    dims, x_hbm, c_hbm, mu_hbm, nu_hbm, ao_hbm, act_hbm, flat_hbm, amat_hbm, right_hbm, act_out,
+    xv, cv, st, ct, c32, qv, pv, muv, nuv, aov, actv, from_core, kept, from_y, summed, flat,
+    picked, nu_col, amat_ref, right_ref, act_col, out_sem, x_sem, in_sem, core_send, core_recv, y_send, y_recv, pair_send, pair_recv,
 ):
     groups, owners, slab, rows_dev, nbasis, nact, nsecond, all_rows, chunk, early = dims
     layers = groups // 2
@@ -79,7 +79,7 @@
     small = [
         pltpu.make_async_copy(src, dst, in_sem.at[k])
         for k, (src, dst) in enumerate(
-            ((c_hbm, cv), (mu_hbm, muv), (nu_hbm, nuv), (ao_hbm, aov), (act_hbm, actv))
+            ((c_hbm, cv.at[pl.ds(0, nact), :]), (mu_hbm, muv), (nu_hbm, nuv), (ao_hbm, aov), (act_hbm, actv))
         )
     ]
     small[0].start()
@@ -103,16 +103,21 @@
             barrier, inc=1, device_id=(g, lax.rem(me + d, owners)), device_id_type=MESH
         )
 
+    cv[nact:, :] = jnp.zeros((LANES - nact, nbasis), BF16)
     small[0].wait()
-    ct[...] = jnp.zeros_like(ct)
-    ct[:nact, :nbasis] = cv[...].astype(F32)
-    c32[...] = ct[...].T
-    cpad[...] = c32[:nbasis, :].astype(BF16)
+    for k in range(groups):
+
+        @pl.when(g == k)
+        def _():
+            st[:, :slab] = cv[:nact, k * slab : (k + 1) * slab]
+
 
     def quarter_step(k, carry):
         x_copy(k).wait()
         where = pl.ds(pl.multiple_of(k * chunk, 16), chunk)
-        qv[where, :] = jnp.dot(xv[where, :], cpad[...], preferred_element_type=F32)
+        qv[where, :] = lax.dot_general(
+            xv[where, :], cv[...], (((1,), (1,)), ((), ())), preferred_element_type=F32
+        )
         return carry
 
     def half_part(first, count, fresh):
@@ -124,15 +129,13 @@
                 ],
                 axis=1,
             )
-            part = jnp.dot(slab_t[:, first : first + count], q, preferred_element_type=F32)
+            part = jnp.dot(st[:, first : first + count], q, preferred_element_type=F32)
             for k in range(2):
                 spot = pl.ds(i + k, nact, stride=rows_dev)
                 mine = part[:, k * LANES : (k + 1) * LANES]
                 pv[spot, :] = mine if fresh else pv[spot, :] + mine
 
     lax.fori_loop(0, early, quarter_step, 0)
-    span = -(-slab // 256) * 256
-    slab_t = c32[pl.ds(g * slab, span), :].T[:nact].astype(BF16)
     cut = early * chunk // rows_dev // 256 * 256
     if cut:
         half_part(0, cut, True)
@@ -220,6 +223,9 @@
     for copy in small[1:]:
         copy.wait()
     cols = nsecond * nact
+    ct[...] = jnp.zeros_like(ct)
+    ct[:, :nbasis] = cv[...].astype(F32)
+    c32[...] = ct[...].T
 
     def pick_row(i, carry):
         picked[pl.ds(i, 1), :] = c32[pl.ds(muv[i], 1), :]
@@ -240,18 +246,65 @@
         jnp.where(spread, 1.0, 0.0).astype(BF16),
         preferred_element_type=F32,
     )
-    amat = jnp.where(section == nu_col[:, :1], wide, 0.0).astype(BF16)
-    weights = jnp.concatenate([amat, amat, amat], axis=0)
+    amat_ref[...] = jnp.where(section == nu_col[:, :1], wide, 0.0).astype(BF16)
     act_wide = jnp.sum(
         jnp.where(spread, act_col[:, :1].astype(F32), 0.0), axis=0, keepdims=True
     ).astype(jnp.int32)
     ao_wide = jnp.zeros((1, cols), jnp.int32)
     for n in range(nsecond):
         ao_wide = jnp.where(section == n, aov[n], ao_wide)
-    right = jnp.bitwise_xor(act_wide, ao_wide)
+    right_ref[...] = jnp.broadcast_to(jnp.bitwise_xor(act_wide, ao_wide), (8, cols))
+    results = [
+        pltpu.make_async_copy(src, dst, out_sem.at[k])
+        for k, (src, dst) in enumerate(
+            (
+                (flat, flat_hbm),
+                (amat_ref, amat_hbm),
+                (right_ref, right_hbm),
+                (act_col, act_out),
+            )
+        )
+    ]
+    for copy in results[1:]:
+        copy.start()
 
     for d in range(1, owners):
         pair_copy(d).wait_recv()
+    results[0].start()
+    for d in order:
+        for step in range(steps):
+            core_copy(d, step).wait_send()
+            if d:
+                y_copy(d, step).wait_send()
+    for d in range(1, owners):
+        pair_copy(d).wait_send()
+    for copy in results:
+        copy.wait()
+
+
+def finish_kernel(
+    dims, flat_hbm, amat_hbm, right_hbm, act_in, out_hbm,
+    flat, amat_ref, right_ref, act_col, out, in_sem, out_sem,
+):
+    owners, rows_dev, per_owner, nact = dims
+    first = (lax.axis_index("grp") * owners + lax.axis_index("pair")) * per_owner
+    arrived = [
+        pltpu.make_async_copy(src, dst, in_sem.at[k])
+        for k, (src, dst) in enumerate(
+            (
+                (flat_hbm, flat),
+                (amat_hbm, amat_ref),
+                (right_hbm, right_ref),
+                (act_in, act_col),
+            )
+        )
+    ]
+    for copy in arrived:
+        copy.start()
+    for copy in arrived:
+        copy.wait()
+    weights = jnp.concatenate([amat_ref[...]] * 3, axis=0)
+    right = right_ref[:1, :]
     copies = []
     for j in range(per_owner):
         f = jnp.concatenate(
@@ -267,19 +320,12 @@
         low = (rest - mid.astype(F32)).astype(BF16)
         parts = jnp.concatenate([high, mid, low], axis=0).astype(F32).T[:nact].astype(BF16)
         full = jnp.dot(parts, weights, preferred_element_type=F32)
-        p = (g * owners + me) * per_owner + j
+        p = first + j
         left = jnp.bitwise_xor(act_col[:, :1], act_col[pl.ds(p, 1), :1])
         here = pl.ds(j * nact, nact)
         out[here, :] = jnp.where(left == right, full, 0.0)
         copies.append(pltpu.make_async_copy(out.at[here, :], out_hbm.at[here, :], out_sem.at[j]))
         copies[-1].start()
-    for d in order:
-        for step in range(steps):
-            core_copy(d, step).wait_send()
-            if d:
-                y_copy(d, step).wait_send()
-    for d in range(1, owners):
-        pair_copy(d).wait_send()
     for copy in copies:
         copy.wait()
 
@@ -299,20 +345,25 @@
     early = min(nchunks, -(-256 * rows_dev // chunk))
     dims = (groups, owners, slab, rows_dev, nbasis, nact, nsecond, all_rows, chunk, early)
     span = -(-slab // 256) * 256
-    deep = -(-(slab * (groups - 1) + span) // LANES) * LANES
+    deep = -(-nbasis // LANES) * LANES
     x = integrals.transpose(1, 0, 2).reshape(rows, nbasis)
     steps = owners // 2
     hbm = pl.BlockSpec(memory_space=pltpu.HBM)
-    return pl.pallas_call(
+    tables = pl.pallas_call(
         functools.partial(transform_kernel, dims),
-        out_shape=jax.ShapeDtypeStruct((per_owner * nact, cols), F32),
+        out_shape=(
+            jax.ShapeDtypeStruct((grows, LANES), F32),
+            jax.ShapeDtypeStruct((all_rows, cols), BF16),
+            jax.ShapeDtypeStruct((8, cols), jnp.int32),
+            jax.ShapeDtypeStruct((nact, LANES), jnp.int32),
+        ),
         in_specs=[hbm] * 6,
-        out_specs=hbm,
+        out_specs=(hbm,) * 4,
         scratch_shapes=[
             pltpu.VMEM((rows, nbasis), BF16),
-            pltpu.VMEM((nact, nbasis), BF16),
+            pltpu.VMEM((LANES, nbasis), BF16),
+            pltpu.VMEM((nact, span), BF16),
             pltpu.VMEM((LANES, deep), F32),
-            pltpu.VMEM((nbasis, LANES), BF16),
             pltpu.VMEM((deep, LANES), F32),
             pltpu.VMEM((rows, LANES), F32),
             pltpu.VMEM((nact * rows_dev, LANES), F32),
@@ -327,9 +378,10 @@
             pltpu.VMEM((grows, LANES), F32),
             pltpu.VMEM((all_rows, LANES), F32),
             pltpu.VMEM((all_rows, LANES), jnp.int32),
+            pltpu.VMEM((all_rows, cols), BF16),
+            pltpu.VMEM((8, cols), jnp.int32),
             pltpu.VMEM((nact, LANES), jnp.int32),
-            pltpu.VMEM((per_owner * nact, cols), F32),
-            pltpu.SemaphoreType.DMA((per_owner,)),
+            pltpu.SemaphoreType.DMA((4,)),
             pltpu.SemaphoreType.DMA((nchunks,)),
             pltpu.SemaphoreType.DMA((5,)),
             pltpu.SemaphoreType.DMA((layers, steps)),
@@ -346,6 +398,22 @@
             flops=2 * rows * nbasis * nact, bytes_accessed=rows * nbasis * 2, transcendentals=0
         ),
     )(x, coeff.T, mu_index, nu_index, ao_irrep, act_irrep)
+    return pl.pallas_call(
+        functools.partial(finish_kernel, (owners, rows_dev, per_owner, nact)),
+        out_shape=jax.ShapeDtypeStruct((per_owner * nact, cols), F32),
+        in_specs=[hbm] * 4,
+        out_specs=hbm,
+        scratch_shapes=[
+            pltpu.VMEM((grows, LANES), F32),
+            pltpu.VMEM((all_rows, cols), BF16),
+            pltpu.VMEM((8, cols), jnp.int32),
+            pltpu.VMEM((nact, LANES), jnp.int32),
+            pltpu.VMEM((per_owner * nact, cols), F32),
+            pltpu.SemaphoreType.DMA((4,)),
+            pltpu.SemaphoreType.DMA((per_owner,)),
+        ],
+        compiler_params=pltpu.CompilerParams(vmem_limit_bytes=VMEM_LIMIT),
+    )(*tables)
 
 
 def on_device(integrals, coeff, mu_index, nu_index, ao_irrep, act_irrep):

time: 27.6 us -> 26.8 us (0.971)
  local copies, waits for them, and re-layouts: 2.14 us -> 0 us
  Pallas kernels: 25.3 us -> 26.7 us
    unnamed x1 -> x0, local copies, waits for them, and re-layouts: 2.14 us -> none
    pallas_call x1 -> x2, Pallas kernels: 25.3 us -> 26.7 us  [the longest x1 24.5 us: fast(): pl.pallas_call(functools.partial(transform_kernel, dims), out_shape=(jax....]
where the time goes in v3:
time: 26.8 us; the launch traced here: 26.7 us
  Pallas kernels  26.7 us (100%)
    pallas_call x1, Pallas kernels, fast(): pl.pallas_call(functools.partial(transform_kernel, dims), out_shape=(jax....  24.5 us
    pallas_call x1, Pallas kernels, fast(): pl.pallas_call(functools.partial(finish_kernel, (owners, rows_dev, per_ow...  2.19 us

profile of v3, /device:TPU:0, one launch (start us, length us, event | category | flops | bytes accessed | tf_op | source)
XLA Modules:
  0.0 26.7 jit_solution(14746179487281112266)
XLA Ops:
  0.0 24.5 %shard_map.64 = (f32[192,128]{1,0:T(8,128)}, bf16[64,768]{1,0:T(8,128)(2,1)}, s32[8,768]{1,0:T(8,128)}, s32[96,128]{1,0:T(8,128)}) custom-call(bf16[4000,2000]{1,0:T(8,128)(2,1)} %bitcast.4, bf16[96,2000]{1,0:T(8,128)(2,1)} %bitcast.5, s32[64]{0:T(128)} %mu_hbm.1, s32[64]{0:T(128)} %nu_hbm.1, s32[8]{0:T(128)} %ao_hbm.1, s32[96]{0:T(128)} %act_hbm.1), custom_call_target="tpu_custom_call" | custom-call | flops 1536000000 | bytes 16000000 | tf_op jit(solution)/shard_map/pallas_call | solution.py:352
  24.5 2.2 %shard_map.65 = f32[288,768]{1,0:T(8,128)} custom-call(f32[192,128]{1,0:T(8,128)} %get-tuple-element.9.flat_hbm, bf16[64,768]{1,0:T(8,128)(2,1)} %get-tuple-element.10.amat_hbm, s32[8,768]{1,0:T(8,128)} %get-tuple-element.11.right_hbm, s32[96,128]{1,0:T(8,128)} %get-tuple-element.12.act_in), custom_call_target="tpu_custom_call" | custom-call | tf_op jit(solution)/shard_map/pallas_call | solution.py:401

commit v4 on v3

--- a/solution.py
+++ b/solution.py
@@ -61,10 +61,10 @@
 
 def transform_kernel(
     dims, x_hbm, c_hbm, mu_hbm, nu_hbm, ao_hbm, act_hbm, flat_hbm, amat_hbm, right_hbm, act_out,
-    xv, cv, st, ct, c32, qv, pv, muv, nuv, aov, actv, from_core, kept, from_y, summed, flat,
+    xv, cv, st, cpad, c32, qv, pv, muv, nuv, aov, actv, from_core, kept, from_y, summed, flat,
     picked, nu_col, amat_ref, right_ref, act_col, out_sem, x_sem, in_sem, core_send, core_recv, y_send, y_recv, pair_send, pair_recv,
 ):
-    groups, owners, slab, rows_dev, nbasis, nact, nsecond, all_rows, chunk, early = dims
+    groups, owners, slab, rows_dev, nbasis, nact, nsecond, all_rows, chunks = dims
     layers = groups // 2
     per_group = nact // groups
     per_owner = per_group // owners
@@ -74,7 +74,6 @@
     me = lax.axis_index("pair")
     y, core = g // 2, g % 2
     other = 1 - core
-    nchunks = slab * rows_dev // chunk
 
     small = [
         pltpu.make_async_copy(src, dst, in_sem.at[k])
@@ -85,10 +84,10 @@
     small[0].start()
 
     def x_copy(k):
-        where = pl.ds(pl.multiple_of(k * chunk, 16), chunk)
+        where = pl.ds(*chunks[k])
         return pltpu.make_async_copy(x_hbm.at[where, :], xv.at[where, :], x_sem.at[k])
 
-    for k in range(nchunks):
+    for k in range(len(chunks)):
         x_copy(k).start()
     for copy in small[1:]:
         copy.start()
@@ -105,20 +104,13 @@
 
     cv[nact:, :] = jnp.zeros((LANES - nact, nbasis), BF16)
     small[0].wait()
-    for k in range(groups):
-
-        @pl.when(g == k)
-        def _():
-            st[:, :slab] = cv[:nact, k * slab : (k + 1) * slab]
-
-
-    def quarter_step(k, carry):
+    cpad[...] = cv[...].T
+
+
+    def quarter_step(k):
         x_copy(k).wait()
-        where = pl.ds(pl.multiple_of(k * chunk, 16), chunk)
-        qv[where, :] = lax.dot_general(
-            xv[where, :], cv[...], (((1,), (1,)), ((), ())), preferred_element_type=F32
-        )
-        return carry
+        where = pl.ds(*chunks[k])
+        qv[where, :] = jnp.dot(xv[where, :], cpad[...], preferred_element_type=F32)
 
     def half_part(first, count, fresh):
         for i in range(0, rows_dev, 2):
@@ -135,11 +127,20 @@
                 mine = part[:, k * LANES : (k + 1) * LANES]
                 pv[spot, :] = mine if fresh else pv[spot, :] + mine
 
-    lax.fori_loop(0, early, quarter_step, 0)
-    cut = early * chunk // rows_dev // 256 * 256
-    if cut:
-        half_part(0, cut, True)
-    lax.fori_loop(early, nchunks, quarter_step, 0)
+    cut = 0
+    for k in range(len(chunks)):
+        quarter_step(k)
+        if k == 0:
+            for part in range(groups):
+
+                @pl.when(g == part)
+                def _():
+                    st[:, :slab] = cv[:nact, part * slab : (part + 1) * slab]
+
+        if k + 2 == len(chunks) - 1:
+            cut = sum(chunks[k]) // rows_dev // 256 * 256
+            if cut:
+                half_part(0, cut, True)
     half_part(cut, slab - cut, not cut)
 
     pl.semaphore_wait(barrier, layers + owners - 1)
@@ -223,9 +224,7 @@
     for copy in small[1:]:
         copy.wait()
     cols = nsecond * nact
-    ct[...] = jnp.zeros_like(ct)
-    ct[:, :nbasis] = cv[...].astype(F32)
-    c32[...] = ct[...].T
+    c32[...] = cpad[...].astype(F32)
 
     def pick_row(i, carry):
         picked[pl.ds(i, 1), :] = c32[pl.ds(muv[i], 1), :]
@@ -340,12 +339,11 @@
     grows = nact // groups * rows_dev
     cols = nsecond * nact
     rows = slab * rows_dev
-    chunk = max(c for c in range(16, 513, 16) if rows % c == 0)
-    nchunks = rows // chunk
-    early = min(nchunks, -(-256 * rows_dev // chunk))
-    dims = (groups, owners, slab, rows_dev, nbasis, nact, nsecond, all_rows, chunk, early)
+    sizes = [rows // 5 // 16 * 16, rows * 8 // 25 // 16 * 16, rows * 8 // 25 // 16 * 16]
+    sizes.append(rows - sum(sizes))
+    chunks = tuple((sum(sizes[:k]), size) for k, size in enumerate(sizes))
+    dims = (groups, owners, slab, rows_dev, nbasis, nact, nsecond, all_rows, chunks)
     span = -(-slab // 256) * 256
-    deep = -(-nbasis // LANES) * LANES
     x = integrals.transpose(1, 0, 2).reshape(rows, nbasis)
     steps = owners // 2
     hbm = pl.BlockSpec(memory_space=pltpu.HBM)
@@ -363,8 +361,8 @@
             pltpu.VMEM((rows, nbasis), BF16),
             pltpu.VMEM((LANES, nbasis), BF16),
             pltpu.VMEM((nact, span), BF16),
-            pltpu.VMEM((LANES, deep), F32),
-            pltpu.VMEM((deep, LANES), F32),
+            pltpu.VMEM((nbasis, LANES), BF16),
+            pltpu.VMEM((nbasis, LANES), F32),
             pltpu.VMEM((rows, LANES), F32),
             pltpu.VMEM((nact * rows_dev, LANES), F32),
             pltpu.SMEM((all_rows,), jnp.int32),
@@ -382,7 +380,7 @@
             pltpu.VMEM((8, cols), jnp.int32),
             pltpu.VMEM((nact, LANES), jnp.int32),
             pltpu.SemaphoreType.DMA((4,)),
-            pltpu.SemaphoreType.DMA((nchunks,)),
+            pltpu.SemaphoreType.DMA((len(chunks),)),
             pltpu.SemaphoreType.DMA((5,)),
             pltpu.SemaphoreType.DMA((layers, steps)),
             pltpu.SemaphoreType.DMA((layers, steps)),

time: 26.8 us -> 28.4 us (1.060)
  Pallas kernels: 26.7 us -> 28.3 us
    pallas_call x1, Pallas kernels: 24.5 us -> 26.1 us  [fast(): pl.pallas_call(functools.partial(transform_kernel, dims), out_shape=(jax....]
where the time goes in v4:
time: 28.4 us; the launch traced here: 28.3 us
  Pallas kernels  28.3 us (100%)
    pallas_call x1, Pallas kernels, fast(): pl.pallas_call(functools.partial(transform_kernel, dims), out_shape=(jax....  26.1 us
    pallas_call x1, Pallas kernels, fast(): pl.pallas_call(functools.partial(finish_kernel, (owners, rows_dev, per_ow...  2.19 us

profile of v4, /device:TPU:0, one launch (start us, length us, event | category | flops | bytes accessed | tf_op | source)
XLA Modules:
  0.0 28.3 jit_solution(13751701237064930489)
XLA Ops:
  0.0 26.1 %shard_map.64 = (f32[192,128]{1,0:T(8,128)}, bf16[64,768]{1,0:T(8,128)(2,1)}, s32[8,768]{1,0:T(8,128)}, s32[96,128]{1,0:T(8,128)}) custom-call(bf16[4000,2000]{1,0:T(8,128)(2,1)} %bitcast.4, bf16[96,2000]{1,0:T(8,128)(2,1)} %bitcast.5, s32[64]{0:T(128)} %mu_hbm.1, s32[64]{0:T(128)} %nu_hbm.1, s32[8]{0:T(128)} %ao_hbm.1, s32[96]{0:T(128)} %act_hbm.1), custom_call_target="tpu_custom_call" | custom-call | flops 1536000000 | bytes 16000000 | tf_op jit(solution)/shard_map/pallas_call | solution.py:350
  26.1 2.2 %shard_map.65 = f32[288,768]{1,0:T(8,128)} custom-call(f32[192,128]{1,0:T(8,128)} %get-tuple-element.9.flat_hbm, bf16[64,768]{1,0:T(8,128)(2,1)} %get-tuple-element.10.amat_hbm, s32[8,768]{1,0:T(8,128)} %get-tuple-element.11.right_hbm, s32[96,128]{1,0:T(8,128)} %get-tuple-element.12.act_in), custom_call_target="tpu_custom_call" | custom-call | tf_op jit(solution)/shard_map/pallas_call | solution.py:399

commit v5 on v3

--- a/solution.py
+++ b/solution.py
@@ -61,7 +61,7 @@
 
 def transform_kernel(
     dims, x_hbm, c_hbm, mu_hbm, nu_hbm, ao_hbm, act_hbm, flat_hbm, amat_hbm, right_hbm, act_out,
-    xv, cv, st, ct, c32, qv, pv, muv, nuv, aov, actv, from_core, kept, from_y, summed, flat,
+    xv, cv, st, cpad, c32, qv, pv, muv, nuv, aov, actv, from_core, kept, from_y, summed, flat,
     picked, nu_col, amat_ref, right_ref, act_col, out_sem, x_sem, in_sem, core_send, core_recv, y_send, y_recv, pair_send, pair_recv,
 ):
     groups, owners, slab, rows_dev, nbasis, nact, nsecond, all_rows, chunk, early = dims
@@ -105,19 +105,13 @@
 
     cv[nact:, :] = jnp.zeros((LANES - nact, nbasis), BF16)
     small[0].wait()
-    for k in range(groups):
-
-        @pl.when(g == k)
-        def _():
-            st[:, :slab] = cv[:nact, k * slab : (k + 1) * slab]
+    cpad[...] = cv[...].T
 
 
     def quarter_step(k, carry):
         x_copy(k).wait()
         where = pl.ds(pl.multiple_of(k * chunk, 16), chunk)
-        qv[where, :] = lax.dot_general(
-            xv[where, :], cv[...], (((1,), (1,)), ((), ())), preferred_element_type=F32
-        )
+        qv[where, :] = jnp.dot(xv[where, :], cpad[...], preferred_element_type=F32)
         return carry
 
     def half_part(first, count, fresh):
@@ -136,6 +130,12 @@
                 pv[spot, :] = mine if fresh else pv[spot, :] + mine
 
     lax.fori_loop(0, early, quarter_step, 0)
+    for part in range(groups):
+
+        @pl.when(g == part)
+        def _():
+            st[:, :slab] = cv[:nact, part * slab : (part + 1) * slab]
+
     cut = early * chunk // rows_dev // 256 * 256
     if cut:
         half_part(0, cut, True)
@@ -223,9 +223,7 @@
     for copy in small[1:]:
         copy.wait()
     cols = nsecond * nact
-    ct[...] = jnp.zeros_like(ct)
-    ct[:, :nbasis] = cv[...].astype(F32)
-    c32[...] = ct[...].T
+    c32[...] = cpad[...].astype(F32)
 
     def pick_row(i, carry):
         picked[pl.ds(i, 1), :] = c32[pl.ds(muv[i], 1), :]
@@ -340,12 +338,11 @@
     grows = nact // groups * rows_dev
     cols = nsecond * nact
     rows = slab * rows_dev
-    chunk = max(c for c in range(16, 513, 16) if rows % c == 0)
+    chunk = max(c for c in range(16, 401, 16) if rows % c == 0)
     nchunks = rows // chunk
     early = min(nchunks, -(-256 * rows_dev // chunk))
     dims = (groups, owners, slab, rows_dev, nbasis, nact, nsecond, all_rows, chunk, early)
     span = -(-slab // 256) * 256
-    deep = -(-nbasis // LANES) * LANES
     x = integrals.transpose(1, 0, 2).reshape(rows, nbasis)
     steps = owners // 2
     hbm = pl.BlockSpec(memory_space=pltpu.HBM)
@@ -363,8 +360,8 @@
             pltpu.VMEM((rows, nbasis), BF16),
             pltpu.VMEM((LANES, nbasis), BF16),
             pltpu.VMEM((nact, span), BF16),
-            pltpu.VMEM((LANES, deep), F32),
-            pltpu.VMEM((deep, LANES), F32),
+            pltpu.VMEM((nbasis, LANES), BF16),
+            pltpu.VMEM((nbasis, LANES), F32),
             pltpu.VMEM((rows, LANES), F32),
             pltpu.VMEM((nact * rows_dev, LANES), F32),
             pltpu.SMEM((all_rows,), jnp.int32),

time: 26.8 us -> 27.1 us (1.011)
  no operation moved by 1% of the time
where the time goes in v5:
time: 27.1 us; the launch traced here: 26.9 us
  Pallas kernels  26.9 us (99%)
    pallas_call x1, Pallas kernels, fast(): pl.pallas_call(functools.partial(transform_kernel, dims), out_shape=(jax....  24.7 us
    pallas_call x1, Pallas kernels, fast(): pl.pallas_call(functools.partial(finish_kernel, (owners, rows_dev, per_ow...  2.19 us

profile of v5, /device:TPU:0, one launch (start us, length us, event | category | flops | bytes accessed | tf_op | source)
XLA Modules:
  0.0 26.9 jit_solution(5190057949835191489)
XLA Ops:
  0.0 24.7 %shard_map.64 = (f32[192,128]{1,0:T(8,128)}, bf16[64,768]{1,0:T(8,128)(2,1)}, s32[8,768]{1,0:T(8,128)}, s32[96,128]{1,0:T(8,128)}) custom-call(bf16[4000,2000]{1,0:T(8,128)(2,1)} %bitcast.4, bf16[96,2000]{1,0:T(8,128)(2,1)} %bitcast.5, s32[64]{0:T(128)} %mu_hbm.1, s32[64]{0:T(128)} %nu_hbm.1, s32[8]{0:T(128)} %ao_hbm.1, s32[96]{0:T(128)} %act_hbm.1), custom_call_target="tpu_custom_call" | custom-call | flops 1536000000 | bytes 16000000 | tf_op jit(solution)/shard_map/pallas_call | solution.py:349
  24.8 2.2 %shard_map.65 = f32[288,768]{1,0:T(8,128)} custom-call(f32[192,128]{1,0:T(8,128)} %get-tuple-element.9.flat_hbm, bf16[64,768]{1,0:T(8,128)(2,1)} %get-tuple-element.10.amat_hbm, s32[8,768]{1,0:T(8,128)} %get-tuple-element.11.right_hbm, s32[96,128]{1,0:T(8,128)} %get-tuple-element.12.act_in), custom_call_target="tpu_custom_call" | custom-call | tf_op jit(solution)/shard_map/pallas_call | solution.py:398

commit v6 on v5

--- a/solution.py
+++ b/solution.py
@@ -11,6 +11,7 @@
 F32 = jnp.float32
 BF16 = jnp.bfloat16
 LANES = 128
+AHEAD = 3
 VMEM_LIMIT = 64 * 1024 * 1024
 
 
@@ -88,7 +89,7 @@
         where = pl.ds(pl.multiple_of(k * chunk, 16), chunk)
         return pltpu.make_async_copy(x_hbm.at[where, :], xv.at[where, :], x_sem.at[k])
 
-    for k in range(nchunks):
+    for k in range(min(AHEAD, nchunks)):
         x_copy(k).start()
     for copy in small[1:]:
         copy.start()
@@ -110,6 +111,11 @@
 
     def quarter_step(k, carry):
         x_copy(k).wait()
+
+        @pl.when(k + AHEAD < nchunks)
+        def _():
+            x_copy(k + AHEAD).start()
+
         where = pl.ds(pl.multiple_of(k * chunk, 16), chunk)
         qv[where, :] = jnp.dot(xv[where, :], cpad[...], preferred_element_type=F32)
         return carry

time: 27.1 us -> 25 us (0.923)
  Pallas kernels: 26.9 us -> 24.9 us
    pallas_call x1, Pallas kernels: 24.7 us -> 22.7 us  [fast(): pl.pallas_call(functools.partial(transform_kernel, dims), out_shape=(jax....]
where the time goes in v6:
time: 25 us; the launch traced here: 24.9 us
  Pallas kernels  24.9 us (100%)
    pallas_call x1, Pallas kernels, fast(): pl.pallas_call(functools.partial(transform_kernel, dims), out_shape=(jax....  22.7 us
    pallas_call x1, Pallas kernels, fast(): pl.pallas_call(functools.partial(finish_kernel, (owners, rows_dev, per_ow...  2.19 us

profile of v6, /device:TPU:0, one launch (start us, length us, event | category | flops | bytes accessed | tf_op | source)
XLA Modules:
  0.0 24.9 jit_solution(9130318273125993967)
XLA Ops:
  0.0 22.7 %shard_map.64 = (f32[192,128]{1,0:T(8,128)}, bf16[64,768]{1,0:T(8,128)(2,1)}, s32[8,768]{1,0:T(8,128)}, s32[96,128]{1,0:T(8,128)}) custom-call(bf16[4000,2000]{1,0:T(8,128)(2,1)} %bitcast.4, bf16[96,2000]{1,0:T(8,128)(2,1)} %bitcast.5, s32[64]{0:T(128)} %mu_hbm.1, s32[64]{0:T(128)} %nu_hbm.1, s32[8]{0:T(128)} %ao_hbm.1, s32[96]{0:T(128)} %act_hbm.1), custom_call_target="tpu_custom_call" | custom-call | flops 1536000000 | bytes 16000000 | tf_op jit(solution)/shard_map/pallas_call | solution.py:355
  22.7 2.2 %shard_map.65 = f32[288,768]{1,0:T(8,128)} custom-call(f32[192,128]{1,0:T(8,128)} %get-tuple-element.9.flat_hbm, bf16[64,768]{1,0:T(8,128)(2,1)} %get-tuple-element.10.amat_hbm, s32[8,768]{1,0:T(8,128)} %get-tuple-element.11.right_hbm, s32[96,128]{1,0:T(8,128)} %get-tuple-element.12.act_in), custom_call_target="tpu_custom_call" | custom-call | tf_op jit(solution)/shard_map/pallas_call | solution.py:404

commit v7 on v6

--- a/solution.py
+++ b/solution.py
@@ -11,7 +11,7 @@
 F32 = jnp.float32
 BF16 = jnp.bfloat16
 LANES = 128
-AHEAD = 3
+AHEAD = 2
 VMEM_LIMIT = 64 * 1024 * 1024
 
 

time: 25 us -> 26.1 us (1.044)
  Pallas kernels: 24.9 us -> 26 us
    pallas_call x1, Pallas kernels: 22.7 us -> 23.8 us  [fast(): pl.pallas_call(functools.partial(transform_kernel, dims), out_shape=(jax....]
where the time goes in v7:
time: 26.1 us; the launch traced here: 26 us
  Pallas kernels  26 us (100%)
    pallas_call x1, Pallas kernels, fast(): pl.pallas_call(functools.partial(transform_kernel, dims), out_shape=(jax....  23.8 us
    pallas_call x1, Pallas kernels, fast(): pl.pallas_call(functools.partial(finish_kernel, (owners, rows_dev, per_ow...  2.19 us

profile of v7, /device:TPU:0, one launch (start us, length us, event | category | flops | bytes accessed | tf_op | source)
XLA Modules:
  0.0 26.0 jit_solution(10679901340664917415)
XLA Ops:
  0.0 23.8 %shard_map.64 = (f32[192,128]{1,0:T(8,128)}, bf16[64,768]{1,0:T(8,128)(2,1)}, s32[8,768]{1,0:T(8,128)}, s32[96,128]{1,0:T(8,128)}) custom-call(bf16[4000,2000]{1,0:T(8,128)(2,1)} %bitcast.4, bf16[96,2000]{1,0:T(8,128)(2,1)} %bitcast.5, s32[64]{0:T(128)} %mu_hbm.1, s32[64]{0:T(128)} %nu_hbm.1, s32[8]{0:T(128)} %ao_hbm.1, s32[96]{0:T(128)} %act_hbm.1), custom_call_target="tpu_custom_call" | custom-call | flops 1536000000 | bytes 16000000 | tf_op jit(solution)/shard_map/pallas_call | solution.py:355
  23.8 2.2 %shard_map.65 = f32[288,768]{1,0:T(8,128)} custom-call(f32[192,128]{1,0:T(8,128)} %get-tuple-element.9.flat_hbm, bf16[64,768]{1,0:T(8,128)(2,1)} %get-tuple-element.10.amat_hbm, s32[8,768]{1,0:T(8,128)} %get-tuple-element.11.right_hbm, s32[96,128]{1,0:T(8,128)} %get-tuple-element.12.act_in), custom_call_target="tpu_custom_call" | custom-call | tf_op jit(solution)/shard_map/pallas_call | solution.py:404
